TPU v7x, 32 devices: a whole 2x2x4 slice. The times are simulated.
32 devices in a mesh: dp: 8 (over z, x), walk: 4 (over y, core).
Axes of the slice: x: 2, y: 2, z: 4, core: 2. Of those that a mesh axis runs over, the one named last changes fastest.
Arguments:
- fields: float32 [512, 65536], P('walk', 'dp'), may hold values from -6 to 6
- sensitivity: bfloat16 [256, 16, 128, 128], P('dp'), may hold values from -0.125 to 0.125
- tile_index: int32 [256, 16], P('dp'), may hold values from 0 to 511
- tile_count: int32 [256], P('dp'), may hold values from 1 to 16, as said below
- observed: float32 [32768], P('dp'), may hold values from -6 to 6
- precision: float32 [32768], P('dp'), may hold values from 0.2 to 4
Outputs:
- fields_next: float32 [512, 65536], P('walk', 'dp')
Inputs may be any that keep to these rules, and one draw needn't show every extreme that they name: `tile_count`: every block of rows uses between 1 and 16 slots, and some block uses all 16; slots at or past the count are ignored.
All inputs are finite; a program needn't handle non-finite values.
Results may differ from a plain program's by a relative error of at most 0.0023.
Values may be sent and summed in bfloat16 or wider, within the bound.
A program may use at most 128 MiB of HBM per device.

v0:
```python
import jax
import jax.numpy as jnp
from jax import lax
from jax.sharding import PartitionSpec as P

WALKERS = 512


def forward(gathered, sensitivity, tile_index, tile_count):
    walkers_here = gathered.shape[0]
    nblocks = sensitivity.shape[0]
    tile_rows = sensitivity.shape[2]
    cell_blocks = gathered.reshape(walkers_here, -1, tile_rows)
    most_live = jnp.max(tile_count)

    def one_slot(slot_id, totals):
        columns = lax.dynamic_index_in_dim(tile_index, slot_id, 1, keepdims=False)
        blocks = jnp.take(cell_blocks, columns, axis=1)
        sensitive = lax.dynamic_index_in_dim(sensitivity, slot_id, 1, keepdims=False)
        product = jnp.einsum("brc,wbc->wbr", sensitive, blocks, preferred_element_type=jnp.float32)
        alive_mask = (slot_id < tile_count)[None, :, None]
        return totals + jnp.where(alive_mask, product, jnp.float32(0.0))

    start_sum = jnp.zeros((walkers_here, nblocks, tile_rows), jnp.float32)
    totals = lax.fori_loop(0, most_live, one_slot, start_sum)
    return totals.reshape(walkers_here, nblocks * tile_rows)


def local(fields, sensitivity, tile_index, tile_count, observed, precision):
    field_bf = fields.astype(jnp.bfloat16)
    gathered = lax.all_gather(field_bf, "dp", axis=1, tiled=True)
    predicted = forward(gathered, sensitivity, tile_index, tile_count)
    pred_sum = lax.psum(jnp.sum(predicted, axis=0), "walk")
    pred_mean = pred_sum / WALKERS
    deviation = (predicted - pred_mean[None, :]).astype(jnp.bfloat16)
    misfit = (precision[None, :] * (predicted - observed[None, :])).astype(jnp.bfloat16)
    partial_rows = lax.dot_general(
        misfit,
        lax.all_gather(deviation, "walk", axis=0, tiled=True),
        (((1,), (1,)), ((), ())),
        preferred_element_type=jnp.float32,
    )
    coupling_mine = lax.psum(partial_rows, "dp") / WALKERS
    squares = lax.psum(jnp.sum(coupling_mine * coupling_mine), "walk")
    spread = jnp.sqrt(squares / (WALKERS * WALKERS) + 1e-06)
    weights = (8.0 * coupling_mine / (WALKERS * spread)).astype(jnp.bfloat16)
    update = jnp.dot(
        weights,
        lax.all_gather(field_bf, "walk", axis=0, tiled=True),
        preferred_element_type=jnp.float32,
    )
    return fields - update


def solution(mesh):
    placed = (P("walk", "dp"), P("dp", None, None, None), P("dp", None), P("dp"), P("dp"), P("dp"))
    return jax.shard_map(
        local, mesh=mesh, in_specs=placed, out_specs=P("walk", "dp"), check_vma=False
    )
```

profile of v0, /device:TPU:0, one launch (start us, length us, event | category | flops | bytes accessed | tf_op | source)
XLA Modules:
  0.0 632.2 jit_solution(5999888927857076047)
XLA Ops:
  11.9 229.7 %all-gather.4.cloned.1.call-done = bf16[128,65536]{0,1:T(8,128)(2,1)} async-done(((bf16[128,8192]{0,1:T(8,128)(2,1)}), bf16[128,65536]{0,1:T(8,128)(2,1)}) %all-gather.4.cloned.1.call-update) | async-done | bytes 16777232 | tf_op jit(solution)/shard_map/all_gather | solution.py:31
  241.7 22.4 %copy.12 = bf16[128,512,128]{2,0,1:T(8,128)(2,1)} copy(bf16[128,512,128]{0,2,1:T(8,128)(2,1)} %bitcast.37) | data formatting | bytes 33554432 | tf_op jit(solution)/shard_map/while | solution.py:25
  264.3 167.2 %while.10 = (s32[]{:T(128)}, f32[128,32,128]{2,0,1:T(8,128)S(1)}, s32[]{:T(128)}, s32[32]{0:T(128)S(1)}, s32[32,16]{0,1:T(8,128)}, /*index=5*/bf16[128,512,128]{...) while((s32[]{:T(128)}, f32[128,32,128]{2,0,1:T(8,128)S(1)}, ...), condition=%wide.region_2.3_spmd, body=%wide.region_1.2_spmd.sunk | while | flops 135791840 | bytes 8393619 | solution.py:25
  265.6 6.5 %gather_fusion = bf16[32,128,128]{2,1,0:T(8,128)(2,1)S(1)} fusion(bf16[128,512,128]{2,0,1:T(8,128)(2,1)} %get-tuple-element.156, s32[1024]{0:T(1024)S(1)} %pad_clamp_fusion.2), kind=kCustom, calls=%fused_computation.clone.1 | custom fusion | bytes 2097280 | tf_op jit(solution)/shard_map/while/body/jit(_take)/gather | solution.py:18
  276.1 6.5 %gather_fusion = bf16[32,128,128]{2,1,0:T(8,128)(2,1)S(1)} fusion(bf16[128,512,128]{2,0,1:T(8,128)(2,1)} %get-tuple-element.156, s32[1024]{0:T(1024)S(1)} %pad_clamp_fusion.2), kind=kCustom, calls=%fused_computation.clone.1 | custom fusion | bytes 2097280 | tf_op jit(solution)/shard_map/while/body/jit(_take)/gather | solution.py:18
  286.5 6.5 %gather_fusion = bf16[32,128,128]{2,1,0:T(8,128)(2,1)S(1)} fusion(bf16[128,512,128]{2,0,1:T(8,128)(2,1)} %get-tuple-element.156, s32[1024]{0:T(1024)S(1)} %pad_clamp_fusion.2), kind=kCustom, calls=%fused_computation.clone.1 | custom fusion | bytes 2097280 | tf_op jit(solution)/shard_map/while/body/jit(_take)/gather | solution.py:18
  296.9 6.5 %gather_fusion = bf16[32,128,128]{2,1,0:T(8,128)(2,1)S(1)} fusion(bf16[128,512,128]{2,0,1:T(8,128)(2,1)} %get-tuple-element.156, s32[1024]{0:T(1024)S(1)} %pad_clamp_fusion.2), kind=kCustom, calls=%fused_computation.clone.1 | custom fusion | bytes 2097280 | tf_op jit(solution)/shard_map/while/body/jit(_take)/gather | solution.py:18
  307.3 6.5 %gather_fusion = bf16[32,128,128]{2,1,0:T(8,128)(2,1)S(1)} fusion(bf16[128,512,128]{2,0,1:T(8,128)(2,1)} %get-tuple-element.156, s32[1024]{0:T(1024)S(1)} %pad_clamp_fusion.2), kind=kCustom, calls=%fused_computation.clone.1 | custom fusion | bytes 2097280 | tf_op jit(solution)/shard_map/while/body/jit(_take)/gather | solution.py:18
  317.7 6.5 %gather_fusion = bf16[32,128,128]{2,1,0:T(8,128)(2,1)S(1)} fusion(bf16[128,512,128]{2,0,1:T(8,128)(2,1)} %get-tuple-element.156, s32[1024]{0:T(1024)S(1)} %pad_clamp_fusion.2), kind=kCustom, calls=%fused_computation.clone.1 | custom fusion | bytes 2097280 | tf_op jit(solution)/shard_map/while/body/jit(_take)/gather | solution.py:18
  328.1 6.5 %gather_fusion = bf16[32,128,128]{2,1,0:T(8,128)(2,1)S(1)} fusion(bf16[128,512,128]{2,0,1:T(8,128)(2,1)} %get-tuple-element.156, s32[1024]{0:T(1024)S(1)} %pad_clamp_fusion.2), kind=kCustom, calls=%fused_computation.clone.1 | custom fusion | bytes 2097280 | tf_op jit(solution)/shard_map/while/body/jit(_take)/gather | solution.py:18
  338.5 6.5 %gather_fusion = bf16[32,128,128]{2,1,0:T(8,128)(2,1)S(1)} fusion(bf16[128,512,128]{2,0,1:T(8,128)(2,1)} %get-tuple-element.156, s32[1024]{0:T(1024)S(1)} %pad_clamp_fusion.2), kind=kCustom, calls=%fused_computation.clone.1 | custom fusion | bytes 2097280 | tf_op jit(solution)/shard_map/while/body/jit(_take)/gather | solution.py:18
  348.9 6.5 %gather_fusion = bf16[32,128,128]{2,1,0:T(8,128)(2,1)S(1)} fusion(bf16[128,512,128]{2,0,1:T(8,128)(2,1)} %get-tuple-element.156, s32[1024]{0:T(1024)S(1)} %pad_clamp_fusion.2), kind=kCustom, calls=%fused_computation.clone.1 | custom fusion | bytes 2097280 | tf_op jit(solution)/shard_map/while/body/jit(_take)/gather | solution.py:18
  359.3 6.5 %gather_fusion = bf16[32,128,128]{2,1,0:T(8,128)(2,1)S(1)} fusion(bf16[128,512,128]{2,0,1:T(8,128)(2,1)} %get-tuple-element.156, s32[1024]{0:T(1024)S(1)} %pad_clamp_fusion.2), kind=kCustom, calls=%fused_computation.clone.1 | custom fusion | bytes 2097280 | tf_op jit(solution)/shard_map/while/body/jit(_take)/gather | solution.py:18
  369.7 6.5 %gather_fusion = bf16[32,128,128]{2,1,0:T(8,128)(2,1)S(1)} fusion(bf16[128,512,128]{2,0,1:T(8,128)(2,1)} %get-tuple-element.156, s32[1024]{0:T(1024)S(1)} %pad_clamp_fusion.2), kind=kCustom, calls=%fused_computation.clone.1 | custom fusion | bytes 2097280 | tf_op jit(solution)/shard_map/while/body/jit(_take)/gather | solution.py:18
  380.1 6.5 %gather_fusion = bf16[32,128,128]{2,1,0:T(8,128)(2,1)S(1)} fusion(bf16[128,512,128]{2,0,1:T(8,128)(2,1)} %get-tuple-element.156, s32[1024]{0:T(1024)S(1)} %pad_clamp_fusion.2), kind=kCustom, calls=%fused_computation.clone.1 | custom fusion | bytes 2097280 | tf_op jit(solution)/shard_map/while/body/jit(_take)/gather | solution.py:18
  390.5 6.5 %gather_fusion = bf16[32,128,128]{2,1,0:T(8,128)(2,1)S(1)} fusion(bf16[128,512,128]{2,0,1:T(8,128)(2,1)} %get-tuple-element.156, s32[1024]{0:T(1024)S(1)} %pad_clamp_fusion.2), kind=kCustom, calls=%fused_computation.clone.1 | custom fusion | bytes 2097280 | tf_op jit(solution)/shard_map/while/body/jit(_take)/gather | solution.py:18
  401.0 6.5 %gather_fusion = bf16[32,128,128]{2,1,0:T(8,128)(2,1)S(1)} fusion(bf16[128,512,128]{2,0,1:T(8,128)(2,1)} %get-tuple-element.156, s32[1024]{0:T(1024)S(1)} %pad_clamp_fusion.2), kind=kCustom, calls=%fused_computation.clone.1 | custom fusion | bytes 2097280 | tf_op jit(solution)/shard_map/while/body/jit(_take)/gather | solution.py:18
  411.4 6.5 %gather_fusion = bf16[32,128,128]{2,1,0:T(8,128)(2,1)S(1)} fusion(bf16[128,512,128]{2,0,1:T(8,128)(2,1)} %get-tuple-element.156, s32[1024]{0:T(1024)S(1)} %pad_clamp_fusion.2), kind=kCustom, calls=%fused_computation.clone.1 | custom fusion | bytes 2097280 | tf_op jit(solution)/shard_map/while/body/jit(_take)/gather | solution.py:18
  421.8 6.5 %gather_fusion = bf16[32,128,128]{2,1,0:T(8,128)(2,1)S(1)} fusion(bf16[128,512,128]{2,0,1:T(8,128)(2,1)} %get-tuple-element.156, s32[1024]{0:T(1024)S(1)} %pad_clamp_fusion.2), kind=kCustom, calls=%fused_computation.clone.1 | custom fusion | bytes 2097280 | tf_op jit(solution)/shard_map/while/body/jit(_take)/gather | solution.py:18
  433.5 10.5 %psum.21 = f32[4096]{0:T(1024)S(1)} all-reduce(f32[4096]{0:T(1024)S(1)} %bitcast.38), channel_id=1, replica_groups=mesh['dp'=8,'walk'=4] {'walk'}, use_global_device_ids=true, to_apply=%region_4.5 | all-reduce | flops 4096 | bytes 32768 | tf_op jit(solution)/shard_map/psum | solution.py:33
  448.5 33.1 %all-gather.6.cloned.1.call-done = bf16[512,4096]{0,1:T(8,128)(2,1)} async-done(((bf16[128,4096]{0,1:T(8,128)(2,1)}), bf16[512,4096]{0,1:T(8,128)(2,1)}) %all-gather.6.cloned.1.call-update) | async-done | bytes 4194320 | tf_op jit(solution)/shard_map/all_gather | solution.py:39
  485.8 70.1 %all-reduce.2.cloned.1.call-done = f32[128,512]{1,0:T(8,128)} async-done(((f32[128,512]{1,0:T(8,128)}), f32[128,512]{1,0:T(8,128)}) %all-reduce.2.cloned.1.call-update) | async-done | bytes 262160 | tf_op jit(solution)/shard_map/psum | solution.py:43
  564.5 51.7 %all-gather.8.cloned.1.call-done = bf16[512,8192]{0,1:T(8,128)(2,1)} async-done(((bf16[128,8192]{0,1:T(8,128)(2,1)}), bf16[512,8192]{0,1:T(8,128)(2,1)}) %all-gather.8.cloned.1.call-update) | async-done | bytes 8388624 | tf_op jit(solution)/shard_map/all_gather | solution.py:49
  616.2 9.5 %convolution_subtract_fusion = f32[128,8192]{1,0:T(8,128)} fusion(f32[128,8192]{1,0:T(8,128)} %param.8, bf16[512,8192]{0,1:T(8,128)(2,1)} %all-gather.8.cloned.1.call-done, f32[128,512]{1,0:T(8,128)} %all-reduce.2.cloned.1.call-done, f32[]{:T(128)S(6)} %mul.25), kind=kOutput, calls=%fused_computation.14 | convolution fusion | flops 1074987008 | bytes 17039364 | tf_op jit(solution)/shard_map/dot_general | solution.py:47
  (88 shorter events, 76.1 us)
Async XLA Ops:
  6.5 4.7 copy-start.2
  6.5 235.1 %all-gather.4.cloned.1.call-start = ((), (), s32[]{:S(2)}) async-start(), calls=%async_computation | async-start | bytes 18874368 | tf_op jit(solution)/shard_map/all_gather | solution.py:31
  11.2 470.4 %all-gather.6.cloned.1.call-start = ((), (), s32[]{:S(2)}) async-start(), calls=%async_computation.1 | async-start | bytes 5242880 | tf_op jit(solution)/shard_map/all_gather | solution.py:39
  431.5 12.5 %copy-start = (f32[4096]{0:T(1024)S(1)}, f32[4096]{0:T(1024)}, u32[]{:S(2)}) copy-start(f32[4096]{0:T(1024)} %param.12) | copy-start | bytes 49156
  431.5 12.5 %copy-start.1 = (f32[4096]{0:T(1024)S(1)}, f32[4096]{0:T(1024)}, u32[]{:S(2)}) copy-start(f32[4096]{0:T(1024)} %param.13) | copy-start | bytes 49156
  448.5 107.5 %all-reduce.2.cloned.1.call-start = ((), (), s32[]{:S(2)}) async-start(), calls=%async_computation.2 | async-start | bytes 524288 | tf_op jit(solution)/shard_map/psum | solution.py:43
  485.3 130.9 %all-gather.8.cloned.1.call-start = ((), (), s32[]{:S(2)}) async-start(), calls=%async_computation.3 | async-start | bytes 10485760 | tf_op jit(solution)/shard_map/all_gather | solution.py:49
Sparse Core Ops, SparseCore 0:
  11.3 230.2 all-gather.3
  448.6 32.9 all-gather.5
  485.4 70.5 all-reduce.1
  557.5 58.6 all-gather.7
where the time goes:
time: 635 us; the launch traced here: 632 us
  waiting for transfers between devices  385 us (61%)
  local copies, waits for them, and re-layouts  133 us (21%)
  matrix products  53.6 us (8%)
  other arithmetic  18.3 us (3%)
  blocking collectives  16.7 us (3%)
  between operations  13.8 us (2%)
  loops' own time  11 us (2%)
    all_gather x1, waiting for transfers between devices, local(): gathered = lax.all_gather(field_bf, 'dp', axis=1, tiled=True)  230 us
    gather x16, local copies, waits for them, and re-layouts, one_slot(): blocks = jnp.take(cell_blocks, columns, axis=1)  104 us
    psum x1, waiting for transfers between devices, local(): coupling_mine = lax.psum(partial_rows, 'dp') / WALKERS  70.1 us
    all_gather x1, waiting for transfers between devices, local(): lax.all_gather(field_bf, 'walk', axis=0, tiled=True)  51.7 us
    dot_general x16, matrix products, one_slot(): jnp.einsum('brc,wbc->wbr', sensitive, blocks, preferred_element_type=jnp....  40.4 us
    all_gather x1, waiting for transfers between devices, local(): lax.all_gather(deviation, 'walk', axis=0, tiled=True)  33.1 us
    while x2, local copies, waits for them, and re-layouts, forward(): totals = lax.fori_loop(0, most_live, one_slot, start_sum)  24.3 us
  transfers between devices with their start and end apart: 4, of which 4 were waited for; matrix products, arithmetic and copies ran while one was open for 0% of the time, Pallas kernels for 0%

commit v1 on v0

--- a/solution.py
+++ b/solution.py
@@ -40,7 +40,7 @@
         (((1,), (1,)), ((), ())),
         preferred_element_type=jnp.float32,
     )
-    coupling_mine = lax.psum(partial_rows, "dp") / WALKERS
+    coupling_mine = jnp.sum(lax.all_gather(partial_rows, "dp"), axis=0) / WALKERS
     squares = lax.psum(jnp.sum(coupling_mine * coupling_mine), "walk")
     spread = jnp.sqrt(squares / (WALKERS * WALKERS) + 1e-06)
     weights = (8.0 * coupling_mine / (WALKERS * spread)).astype(jnp.bfloat16)

time: 635 us -> 613 us (0.965)
  waiting for transfers between devices: 385 us -> 362 us
    psum x1 -> x0, waiting for transfers between devices: 70.1 us -> none  [local(): coupling_mine = lax.psum(partial_rows, 'dp') / WALKERS]
    all_gather x0 -> x1, waiting for transfers between devices: none -> 48.9 us  [local(): lax.all_gather(partial_rows, 'dp')]
  transfers between devices with their start and end apart: 4 -> 4, of which waited for: 4 -> 4; matrix products, arithmetic and copies ran while one was open for 0% -> 1% of each run, Pallas kernels for 0% -> 0%
where the time goes in v1:
time: 613 us; the launch traced here: 610 us
  waiting for transfers between devices  362 us (59%)
  local copies, waits for them, and re-layouts  134 us (22%)
  matrix products  53.5 us (9%)
  other arithmetic  19.2 us (3%)
  blocking collectives  16.8 us (3%)
  between operations  13.8 us (2%)
  loops' own time  11 us (2%)
    all_gather x1, waiting for transfers between devices, local(): gathered = lax.all_gather(field_bf, 'dp', axis=1, tiled=True)  229 us
    gather x16, local copies, waits for them, and re-layouts, one_slot(): blocks = jnp.take(cell_blocks, columns, axis=1)  104 us
    all_gather x1, waiting for transfers between devices, local(): lax.all_gather(field_bf, 'walk', axis=0, tiled=True)  49.9 us
    all_gather x1, waiting for transfers between devices, local(): lax.all_gather(partial_rows, 'dp')  48.9 us
    dot_general x16, matrix products, one_slot(): jnp.einsum('brc,wbc->wbr', sensitive, blocks, preferred_element_type=jnp....  40.4 us
    all_gather x1, waiting for transfers between devices, local(): lax.all_gather(deviation, 'walk', axis=0, tiled=True)  33.1 us
    while x2, local copies, waits for them, and re-layouts, forward(): totals = lax.fori_loop(0, most_live, one_slot, start_sum)  24.3 us
  transfers between devices with their start and end apart: 4, of which 4 were waited for; matrix products, arithmetic and copies ran while one was open for 1% of the time, Pallas kernels for 0%

profile of v1, /device:TPU:0, one launch (start us, length us, event | category | flops | bytes accessed | tf_op | source)
XLA Modules:
  0.0 610.0 jit_solution(11276953485882545837)
XLA Ops:
  12.5 229.2 %all-gather.6.cloned.1.call-done = bf16[128,65536]{0,1:T(8,128)(2,1)} async-done(((bf16[128,8192]{0,1:T(8,128)(2,1)}), bf16[128,65536]{0,1:T(8,128)(2,1)}) %all-gather.6.cloned.1.call-update) | async-done | bytes 16777232 | tf_op jit(solution)/shard_map/all_gather | solution.py:31
  241.6 22.4 %copy.16 = bf16[128,512,128]{2,0,1:T(8,128)(2,1)} copy(bf16[128,512,128]{0,2,1:T(8,128)(2,1)} %bitcast.38) | data formatting | bytes 33554432 | tf_op jit(solution)/shard_map/while | solution.py:25
  264.3 167.2 %while.10 = (s32[]{:T(128)}, f32[128,32,128]{2,0,1:T(8,128)S(1)}, s32[]{:T(128)}, s32[32]{0:T(128)S(1)}, s32[32,16]{0,1:T(8,128)}, /*index=5*/bf16[128,512,128]{...) while((s32[]{:T(128)}, f32[128,32,128]{2,0,1:T(8,128)S(1)}, ...), condition=%wide.region_2.3_spmd, body=%wide.region_1.2_spmd.sunk | while | flops 135791840 | bytes 8393619 | solution.py:25
  265.6 6.5 %gather_fusion = bf16[32,128,128]{2,1,0:T(8,128)(2,1)S(1)} fusion(bf16[128,512,128]{2,0,1:T(8,128)(2,1)} %get-tuple-element.163, s32[1024]{0:T(1024)S(1)} %pad_clamp_fusion.2), kind=kCustom, calls=%fused_computation.clone.1 | custom fusion | bytes 2097280 | tf_op jit(solution)/shard_map/while/body/jit(_take)/gather | solution.py:18
  276.0 6.5 %gather_fusion = bf16[32,128,128]{2,1,0:T(8,128)(2,1)S(1)} fusion(bf16[128,512,128]{2,0,1:T(8,128)(2,1)} %get-tuple-element.163, s32[1024]{0:T(1024)S(1)} %pad_clamp_fusion.2), kind=kCustom, calls=%fused_computation.clone.1 | custom fusion | bytes 2097280 | tf_op jit(solution)/shard_map/while/body/jit(_take)/gather | solution.py:18
  286.5 6.5 %gather_fusion = bf16[32,128,128]{2,1,0:T(8,128)(2,1)S(1)} fusion(bf16[128,512,128]{2,0,1:T(8,128)(2,1)} %get-tuple-element.163, s32[1024]{0:T(1024)S(1)} %pad_clamp_fusion.2), kind=kCustom, calls=%fused_computation.clone.1 | custom fusion | bytes 2097280 | tf_op jit(solution)/shard_map/while/body/jit(_take)/gather | solution.py:18
  296.9 6.5 %gather_fusion = bf16[32,128,128]{2,1,0:T(8,128)(2,1)S(1)} fusion(bf16[128,512,128]{2,0,1:T(8,128)(2,1)} %get-tuple-element.163, s32[1024]{0:T(1024)S(1)} %pad_clamp_fusion.2), kind=kCustom, calls=%fused_computation.clone.1 | custom fusion | bytes 2097280 | tf_op jit(solution)/shard_map/while/body/jit(_take)/gather | solution.py:18
  307.3 6.5 %gather_fusion = bf16[32,128,128]{2,1,0:T(8,128)(2,1)S(1)} fusion(bf16[128,512,128]{2,0,1:T(8,128)(2,1)} %get-tuple-element.163, s32[1024]{0:T(1024)S(1)} %pad_clamp_fusion.2), kind=kCustom, calls=%fused_computation.clone.1 | custom fusion | bytes 2097280 | tf_op jit(solution)/shard_map/while/body/jit(_take)/gather | solution.py:18
  317.7 6.5 %gather_fusion = bf16[32,128,128]{2,1,0:T(8,128)(2,1)S(1)} fusion(bf16[128,512,128]{2,0,1:T(8,128)(2,1)} %get-tuple-element.163, s32[1024]{0:T(1024)S(1)} %pad_clamp_fusion.2), kind=kCustom, calls=%fused_computation.clone.1 | custom fusion | bytes 2097280 | tf_op jit(solution)/shard_map/while/body/jit(_take)/gather | solution.py:18
  328.1 6.5 %gather_fusion = bf16[32,128,128]{2,1,0:T(8,128)(2,1)S(1)} fusion(bf16[128,512,128]{2,0,1:T(8,128)(2,1)} %get-tuple-element.163, s32[1024]{0:T(1024)S(1)} %pad_clamp_fusion.2), kind=kCustom, calls=%fused_computation.clone.1 | custom fusion | bytes 2097280 | tf_op jit(solution)/shard_map/while/body/jit(_take)/gather | solution.py:18
  338.5 6.5 %gather_fusion = bf16[32,128,128]{2,1,0:T(8,128)(2,1)S(1)} fusion(bf16[128,512,128]{2,0,1:T(8,128)(2,1)} %get-tuple-element.163, s32[1024]{0:T(1024)S(1)} %pad_clamp_fusion.2), kind=kCustom, calls=%fused_computation.clone.1 | custom fusion | bytes 2097280 | tf_op jit(solution)/shard_map/while/body/jit(_take)/gather | solution.py:18
  348.9 6.5 %gather_fusion = bf16[32,128,128]{2,1,0:T(8,128)(2,1)S(1)} fusion(bf16[128,512,128]{2,0,1:T(8,128)(2,1)} %get-tuple-element.163, s32[1024]{0:T(1024)S(1)} %pad_clamp_fusion.2), kind=kCustom, calls=%fused_computation.clone.1 | custom fusion | bytes 2097280 | tf_op jit(solution)/shard_map/while/body/jit(_take)/gather | solution.py:18
  359.3 6.5 %gather_fusion = bf16[32,128,128]{2,1,0:T(8,128)(2,1)S(1)} fusion(bf16[128,512,128]{2,0,1:T(8,128)(2,1)} %get-tuple-element.163, s32[1024]{0:T(1024)S(1)} %pad_clamp_fusion.2), kind=kCustom, calls=%fused_computation.clone.1 | custom fusion | bytes 2097280 | tf_op jit(solution)/shard_map/while/body/jit(_take)/gather | solution.py:18
  369.7 6.5 %gather_fusion = bf16[32,128,128]{2,1,0:T(8,128)(2,1)S(1)} fusion(bf16[128,512,128]{2,0,1:T(8,128)(2,1)} %get-tuple-element.163, s32[1024]{0:T(1024)S(1)} %pad_clamp_fusion.2), kind=kCustom, calls=%fused_computation.clone.1 | custom fusion | bytes 2097280 | tf_op jit(solution)/shard_map/while/body/jit(_take)/gather | solution.py:18
  380.1 6.5 %gather_fusion = bf16[32,128,128]{2,1,0:T(8,128)(2,1)S(1)} fusion(bf16[128,512,128]{2,0,1:T(8,128)(2,1)} %get-tuple-element.163, s32[1024]{0:T(1024)S(1)} %pad_clamp_fusion.2), kind=kCustom, calls=%fused_computation.clone.1 | custom fusion | bytes 2097280 | tf_op jit(solution)/shard_map/while/body/jit(_take)/gather | solution.py:18
  390.5 6.5 %gather_fusion = bf16[32,128,128]{2,1,0:T(8,128)(2,1)S(1)} fusion(bf16[128,512,128]{2,0,1:T(8,128)(2,1)} %get-tuple-element.163, s32[1024]{0:T(1024)S(1)} %pad_clamp_fusion.2), kind=kCustom, calls=%fused_computation.clone.1 | custom fusion | bytes 2097280 | tf_op jit(solution)/shard_map/while/body/jit(_take)/gather | solution.py:18
  400.9 6.5 %gather_fusion = bf16[32,128,128]{2,1,0:T(8,128)(2,1)S(1)} fusion(bf16[128,512,128]{2,0,1:T(8,128)(2,1)} %get-tuple-element.163, s32[1024]{0:T(1024)S(1)} %pad_clamp_fusion.2), kind=kCustom, calls=%fused_computation.clone.1 | custom fusion | bytes 2097280 | tf_op jit(solution)/shard_map/while/body/jit(_take)/gather | solution.py:18
  411.4 6.5 %gather_fusion = bf16[32,128,128]{2,1,0:T(8,128)(2,1)S(1)} fusion(bf16[128,512,128]{2,0,1:T(8,128)(2,1)} %get-tuple-element.163, s32[1024]{0:T(1024)S(1)} %pad_clamp_fusion.2), kind=kCustom, calls=%fused_computation.clone.1 | custom fusion | bytes 2097280 | tf_op jit(solution)/shard_map/while/body/jit(_take)/gather | solution.py:18
  421.8 6.5 %gather_fusion = bf16[32,128,128]{2,1,0:T(8,128)(2,1)S(1)} fusion(bf16[128,512,128]{2,0,1:T(8,128)(2,1)} %get-tuple-element.163, s32[1024]{0:T(1024)S(1)} %pad_clamp_fusion.2), kind=kCustom, calls=%fused_computation.clone.1 | custom fusion | bytes 2097280 | tf_op jit(solution)/shard_map/while/body/jit(_take)/gather | solution.py:18
  433.5 10.5 %psum.14 = f32[4096]{0:T(1024)S(1)} all-reduce(f32[4096]{0:T(1024)S(1)} %bitcast.40), channel_id=1, replica_groups=mesh['dp'=8,'walk'=4] {'walk'}, use_global_device_ids=true, to_apply=%region_4.5 | all-reduce | flops 4096 | bytes 32768 | tf_op jit(solution)/shard_map/psum | solution.py:33
  448.5 33.1 %all-gather.8.cloned.1.call-done = bf16[512,4096]{0,1:T(8,128)(2,1)} async-done(((bf16[128,4096]{0,1:T(8,128)(2,1)}), bf16[512,4096]{0,1:T(8,128)(2,1)}) %all-gather.8.cloned.1.call-update) | async-done | bytes 4194320 | tf_op jit(solution)/shard_map/all_gather | solution.py:39
  485.8 48.9 %all-gather.12.cloned.1.call-done = f32[1024,512]{1,0:T(8,128)} async-done(((f32[128,512]{1,0:T(8,128)}), f32[1024,512]{1,0:T(8,128)}) %all-gather.12.cloned.1.call-update) | async-done | bytes 2097168 | tf_op jit(solution)/shard_map/all_gather | solution.py:43
  544.2 49.9 %all-gather.10.cloned.1.call-done = bf16[512,8192]{0,1:T(8,128)(2,1)} async-done(((bf16[128,8192]{0,1:T(8,128)(2,1)}), bf16[512,8192]{0,1:T(8,128)(2,1)}) %all-gather.10.cloned.1.call-update) | async-done | bytes 8388624 | tf_op jit(solution)/shard_map/all_gather | solution.py:49
  594.0 9.4 %convolution_subtract_fusion = f32[128,8192]{1,0:T(8,128)} fusion(f32[128,8192]{1,0:T(8,128)} %param.8, bf16[512,8192]{0,1:T(8,128)(2,1)} %all-gather.10.cloned.1.call-done, f32[128,512]{1,0:T(8,128)S(1)} %reduce_sum.31, f32[]{:T(128)S(6)} %mul.25), kind=kOutput, calls=%fused_computation.14 | convolution fusion | flops 1074987008 | bytes 17039364 | tf_op jit(solution)/shard_map/dot_general | solution.py:47
  (89 shorter events, 77.6 us)
Async XLA Ops:
  6.5 235.1 %all-gather.6.cloned.1.call-start = ((), (), s32[]{:S(2)}) async-start(), calls=%async_computation | async-start | bytes 18874368 | tf_op jit(solution)/shard_map/all_gather | solution.py:31
  11.2 0.7 copy-start.2
  11.2 470.4 %all-gather.8.cloned.1.call-start = ((), (), s32[]{:S(2)}) async-start(), calls=%async_computation.1 | async-start | bytes 5242880 | tf_op jit(solution)/shard_map/all_gather | solution.py:39
  433.3 10.6 %copy-start = (f32[4096]{0:T(1024)S(1)}, f32[4096]{0:T(1024)}, u32[]{:S(2)}) copy-start(f32[4096]{0:T(1024)} %param.12) | copy-start | bytes 49156
  433.3 10.6 %copy-start.1 = (f32[4096]{0:T(1024)S(1)}, f32[4096]{0:T(1024)}, u32[]{:S(2)}) copy-start(f32[4096]{0:T(1024)} %param.13) | copy-start | bytes 49156
  448.4 86.3 %all-gather.12.cloned.1.call-start = ((), (), s32[]{:S(2)}) async-start(), calls=%async_computation.3 | async-start | bytes 2359296 | tf_op jit(solution)/shard_map/all_gather | solution.py:43
  485.3 108.8 %all-gather.10.cloned.1.call-start = ((), (), s32[]{:S(2)}) async-start(), calls=%async_computation.2 | async-start | bytes 10485760 | tf_op jit(solution)/shard_map/all_gather | solution.py:49
Sparse Core Ops, SparseCore 0:
  11.3 230.2 all-gather.5
  448.6 32.9 all-gather.7
  485.4 49.2 all-gather.11
  536.1 57.8 all-gather.9
